TPU v7x, 32 devices: a whole 2x2x4 slice. The times are simulated.
32 devices in a mesh: row: 8 (over z, y), col: 4 (over x, core).
Axes of the slice: x: 2, y: 2, z: 4, core: 2. Of those that a mesh axis runs over, the one named last changes fastest.
Arguments:
- density: float32 [2, 160, 32, 160, 160], P(None, 'col', None, 'row'), may hold values from -2 to 2
- potential: float32 [160, 160], P('row'), may hold values from 0 to 2
Outputs:
- liouville: float32 [2, 160, 160, 1024], P(None, 'col', 'row')
All inputs are finite; a program needn't handle non-finite values.
Results may differ from a plain program's by a relative error of at most 0.000055.
Values sent between devices are 32-bit elements; how exact they have to be, the bound alone decides.
A program may use at most 384 MiB of HBM per device.

v0:
```python
import jax
import jax.numpy as jnp
from jax import lax
from jax.sharding import PartitionSpec as P

friction = 0.005
diffusion = 0.0001
highest = lax.Precision.HIGHEST


def operators(grid_width):
    positions = jnp.arange(grid_width)
    signed = jnp.where(positions < grid_width // 2, positions, positions - grid_width)
    wavenumber = 2.0 * jnp.pi / grid_width * signed.astype(jnp.float32)
    slope_wave = jnp.where(positions == grid_width // 2, 0.0, wavenumber)
    phases = positions[:, None] * positions[None, :] % grid_width
    angles = 2.0 * jnp.pi / grid_width * phases.astype(jnp.float32)
    kinetic_row = jnp.sum(0.5 * wavenumber * wavenumber * jnp.cos(angles), axis=1) / grid_width
    slope_row = -jnp.sum(slope_wave * jnp.sin(angles), axis=1) / grid_width
    distance = (positions[:, None] - positions[None, :]) % grid_width
    return (kinetic_row[distance], slope_row[distance])


def on_device(density, potential):
    grid_width = density.shape[4]
    window_size = density.shape[2]
    cols_here = density.shape[1]
    rows_here = density.shape[3]
    kinetic, slope_matrix = operators(grid_width)
    matrices = jnp.concatenate([kinetic[:window_size].T, slope_matrix[:window_size].T], axis=1)
    product = jnp.einsum("cpqbx,xe->cpebq", density, matrices, precision=highest)
    kinetic_one = product[:, :, :window_size]
    grad_one = product[:, :, window_size:]
    window_part = jnp.transpose(density[..., :window_size], (0, 1, 4, 3, 2))
    local_potential = potential[:, :window_size].T.reshape(1, 1, window_size, rows_here, 1)
    applied = kinetic_one + local_potential * window_part
    stacked = jnp.concatenate([kinetic, slope_matrix], axis=0)
    row_start = lax.axis_index("row") * rows_here
    col_start = lax.axis_index("col") * cols_here
    offset_one = (jnp.arange(window_size)[:, None] - jnp.arange(window_size)[None, :]).astype(
        jnp.float32
    )
    offset_one = offset_one.reshape(1, 1, window_size, 1, window_size)
    rows_global = (
        (row_start + jnp.arange(rows_here)).astype(jnp.float32).reshape(1, 1, 1, rows_here, 1)
    )
    cols_global = (
        (col_start + jnp.arange(cols_here)).astype(jnp.float32).reshape(1, cols_here, 1, 1, 1)
    )
    offset_two = rows_global - cols_global
    squared = offset_one**2 + offset_two**2
    source = lax.all_to_all(window_part, "row", split_axis=2, concat_axis=3, tiled=True)
    applied_mid = lax.all_to_all(applied, "row", split_axis=2, concat_axis=3, tiled=True)
    grad_mid = lax.all_to_all(grad_one, "row", split_axis=2, concat_axis=3, tiled=True)
    paired = jnp.einsum("capbq,eb->capeq", source, stacked, precision=highest)
    full_applied = applied_mid + paired[:, :, :, :grid_width]
    grad_two = paired[:, :, :, grid_width:]
    applied_back, grad_back = (
        lax.all_to_all(full_applied, "row", split_axis=3, concat_axis=2, tiled=True),
        lax.all_to_all(grad_two, "row", split_axis=3, concat_axis=2, tiled=True),
    )
    mirror_applied, mirror_one, mirror_two = (
        lax.all_to_all(
            lax.all_to_all(full_applied, "col", split_axis=3, concat_axis=1, tiled=True),
            "row",
            split_axis=1,
            concat_axis=2,
            tiled=True,
        ),
        lax.all_to_all(
            lax.all_to_all(grad_mid, "col", split_axis=3, concat_axis=1, tiled=True),
            "row",
            split_axis=1,
            concat_axis=2,
            tiled=True,
        ),
        lax.all_to_all(
            lax.all_to_all(grad_two, "col", split_axis=3, concat_axis=1, tiled=True),
            "row",
            split_axis=1,
            concat_axis=2,
            tiled=True,
        ),
    )
    mirror_applied = jnp.transpose(mirror_applied, (0, 3, 4, 1, 2))
    mirror_one = jnp.transpose(mirror_one, (0, 3, 4, 1, 2))
    mirror_two = jnp.transpose(mirror_two, (0, 3, 4, 1, 2))
    differ_real = applied_back[0] - mirror_applied[0]
    differ_imag = applied_back[1] + mirror_applied[1]
    first_real = grad_one[0] - mirror_one[0]
    first_imag = grad_one[1] + mirror_one[1]
    second_real = grad_back[0] - mirror_two[0]
    second_imag = grad_back[1] + mirror_two[1]
    real_out = differ_imag - friction * (offset_one[0] * first_real + offset_two[0] * second_real)
    imag_out = -differ_real - friction * (offset_one[0] * first_imag + offset_two[0] * second_imag)
    real_out = real_out - diffusion * squared[0] * window_part[0]
    imag_out = imag_out - diffusion * squared[0] * window_part[1]
    result = jnp.stack([real_out, imag_out])
    result = jnp.transpose(result, (0, 1, 3, 4, 2))
    return result.reshape(2, cols_here, rows_here, window_size * window_size)


def solution(mesh):
    in_specs = (P(None, "col", None, "row", None), P("row", None))
    out_specs = P(None, "col", "row", None)
    return jax.shard_map(
        on_device, mesh=mesh, in_specs=in_specs, out_specs=out_specs, check_vma=False
    )
```

profile of v0, /device:TPU:0, one launch (start us, length us, event | category | flops | bytes accessed | tf_op | source)
XLA Modules:
  0.0 2895.3 jit_solution(5164920676413358979)
XLA Ops:
  0.1 46.7 %copy.127 = f32[2,40,32,20,160]{4,1,3,2,0:T(8,128)} copy(f32[2,40,32,20,160]{4,2,3,1,0:T(8,128)} %param.2) | data formatting | bytes 65536000 | tf_op args[0]
  47.8 158.1 %gather_fusion.1 = f32[25600]{0:T(1024)S(1)} fusion(f32[160]{0:T(256)S(1)} %negate_multiply_fusion, s32[25600]{0:T(1024)S(1)} %broadcast_clamp_fusion), kind=kCustom, calls=%fused_computation.1 | custom fusion | bytes 307200 | tf_op jit(solution)/shard_map/gather | solution.py:21
  206.7 158.1 %gather_fusion = f32[25600]{0:T(1024)S(1)} fusion(f32[160]{0:T(256)S(1)} %broadcast_multiply_fusion, s32[25600]{0:T(1024)S(1)} %broadcast_clamp_fusion), kind=kCustom, calls=%fused_computation | custom fusion | bytes 307200 | tf_op jit(solution)/shard_map/gather | solution.py:21
  365.0 75.3 %convolution_bitcast_fusion = f32[2,40,64,20,32]{2,1,3,4,0:T(8,128)} fusion(f32[160,32]{0,1:T(8,128)S(1)} %bitcast.148, f32[160,32]{0,1:T(8,128)S(1)} %bitcast.149, f32[2,40,32,20,160]{4,2,3,1,0:T(8,128)} %param.2), kind=kOutput, calls=%fused_computation.10 | convolution fusion | flops 6291466240 | bytes 45916160 | tf_op jit(solution)/shard_map/cpqbx,xe->cpebq/dot_general | solution.py:31
  440.2 43.1 %slice_add_fusion = (f32[2,40,32,20,32]{2,1,3,4,0:T(8,128)}, f32[2,40,32,20,32]{2,1,3,4,0:T(8,128)}) fusion(f32[2,40,64,20,32]{2,1,3,4,0:T(8,128)} %convolution_bitcast_fusion, f32[32,20]{0,1:T(8,128)S(1)} %slice_bitcast_fusion.1, f32[2,40,32,20,160]{4,1,3,2,0:T(8,128)} %copy.127), kind=kLoop, calls=%fused_computation.3 | loop fusion | flops 3276800 | bytes 32770560 | tf_op jit(solution)/shard_map/add | solution.py:36
  602.4 79.3 %all-to-all-done = f32[8,1,204800]{2,1,0:T(1,128)} async-done(((f32[8,1,204800]{2,1,0:T(1,128)}), f32[8,1,204800]{2,1,0:T(1,128)}, u32[]{:S(2)}, u32[]{:S(2)}) %all-to-all-start) | async-done | bytes 6553632 | tf_op jit(solution)/shard_map/all_to_all | solution.py:53
  733.6 95.8 %all-to-all-done.1 = f32[8,1,204800]{2,1,0:T(1,128)} async-done(((f32[8,1,204800]{2,1,0:T(1,128)}), f32[8,1,204800]{2,1,0:T(1,128)}, u32[]{:S(2)}, u32[]{:S(2)}) %all-to-all-start.1) | async-done | bytes 6553632 | tf_op jit(solution)/shard_map/all_to_all | solution.py:52
  835.1 57.0 %reduce = f32[8,204800]{1,0:T(8,128)} reduce(f32[8,1,204800]{2,1,0:T(1,128)} %all-to-all-done, f32[]{:T(128)} %broadcast.227), dimensions={1}, to_apply=%all_to_all.139.reduce_sub_computation | reduce | bytes 13107204 | tf_op jit(solution)/shard_map/all_to_all | solution.py:53
  955.4 57.0 %reduce.1 = f32[8,204800]{1,0:T(8,128)} reduce(f32[8,1,204800]{2,1,0:T(1,128)} %all-to-all-done.1, f32[]{:T(128)} %broadcast.227), dimensions={1}, to_apply=%all_to_all.143.reduce_sub_computation | reduce | bytes 13107204 | tf_op jit(solution)/shard_map/all_to_all | solution.py:52
  1049.4 43.6 %fusion.15 = f32[2,40,4,320,32]{3,1,4,2,0:T(8,128)} fusion(f32[2,40,4,160,32]{1,4,3,2,0:T(8,128)S(1)} %bitcast.113, f32[160,160]{0,1:T(8,128)S(1)} %copy.133, f32[160,160]{0,1:T(8,128)S(1)} %copy.132), kind=kOutput, calls=%fused_computation.34 | convolution fusion | flops 6291507200 | bytes 19865600 | tf_op jit(solution)/shard_map/capbq,eb->capeq/dot_general | solution.py:55
  1128.3 33.5 %reshape.226 = f32[4,1,409600]{2,1,0:T(1,128)} reshape(f32[160,2,4,32,40]{4,3,2,1,0:T(8,128)} %bitcast.109) | data formatting | bytes 13107200
  1167.2 56.9 %reduce.5 = f32[8,204800]{1,0:T(8,128)} reduce(f32[8,1,204800]{2,1,0:T(1,128)} %all-to-all-done.5, f32[]{:T(128)} %broadcast.227), dimensions={1}, to_apply=%all_to_all.158.reduce_sub_computation | reduce | bytes 13107204 | tf_op jit(solution)/shard_map/all_to_all | solution.py:54
  1268.2 33.5 %reshape.232 = f32[4,1,409600]{2,1,0:T(1,128)} reshape(f32[160,2,4,32,40]{4,3,2,1,0:T(8,128)} %bitcast.126) | data formatting | bytes 13107200
  1325.7 33.3 %reshape.240 = f32[4,1,409600]{2,1,0:T(1,128)} reshape(f32[160,2,4,32,40]{4,3,2,1,0:T(8,128)} %bitcast.111) | data formatting | bytes 13107200
  1408.9 50.6 %all-to-all-done.3 = f32[4,1,409600]{2,1,0:T(1,128)} async-done(((f32[4,1,409600]{2,1,0:T(1,128)}), f32[4,1,409600]{2,1,0:T(1,128)}, u32[]{:S(2)}, u32[]{:S(2)}) %all-to-all-start.3) | async-done | bytes 6553632 | tf_op jit(solution)/shard_map/all_to_all | solution.py:64
  1488.3 120.7 %all-to-all-done.8 = f32[8,1,204800]{2,1,0:T(1,128)} async-done(((f32[8,1,204800]{2,1,0:T(1,128)}), f32[8,1,204800]{2,1,0:T(1,128)}, u32[]{:S(2)}, u32[]{:S(2)}) %all-to-all-start.8) | async-done | bytes 6553632 | tf_op jit(solution)/shard_map/all_to_all | solution.py:60
  1614.2 71.4 %reduce.3 = f32[4,409600]{1,0:T(4,128)} reduce(f32[4,1,409600]{2,1,0:T(1,128)} %all-to-all-done.9, f32[]{:T(128)} %broadcast.227), dimensions={1}, to_apply=%all_to_all.173.reduce_sub_computation | reduce | bytes 13107204 | tf_op jit(solution)/shard_map/all_to_all | solution.py:78
  1685.6 27.3 reshape.227
  1738.4 30.3 %copy.179 = f32[2,4,40,4,40,32]{4,5,3,0,2,1:T(8,128)} copy(f32[2,4,40,4,40,32]{2,1,5,4,3,0:T(4,128)} %bitcast.128) | data formatting | bytes 13107200 | tf_op jit(solution)/shard_map/all_to_all | solution.py:78
  1797.6 71.7 %reduce.6 = f32[4,409600]{1,0:T(4,128)} reduce(f32[4,1,409600]{2,1,0:T(1,128)} %all-to-all-done.6, f32[]{:T(128)} %broadcast.227), dimensions={1}, to_apply=%all_to_all.162.reduce_sub_computation | reduce | bytes 13107204 | tf_op jit(solution)/shard_map/all_to_all | solution.py:71
  1869.4 27.3 reshape.233
  1922.3 30.2 %copy.177 = f32[2,4,40,4,40,32]{4,5,3,0,2,1:T(8,128)} copy(f32[2,4,40,4,40,32]{2,1,5,4,3,0:T(4,128)} %bitcast.131) | data formatting | bytes 13107200 | tf_op jit(solution)/shard_map/all_to_all | solution.py:71
  1981.4 71.8 %reduce.9 = f32[4,409600]{1,0:T(4,128)} reduce(f32[4,1,409600]{2,1,0:T(1,128)} %all-to-all-done.3, f32[]{:T(128)} %broadcast.227), dimensions={1}, to_apply=%all_to_all.150.reduce_sub_computation | reduce | bytes 13107204 | tf_op jit(solution)/shard_map/all_to_all | solution.py:64
  2053.2 27.3 reshape.241
  2106.0 30.3 %copy.174 = f32[2,4,40,4,40,32]{4,5,3,0,2,1:T(8,128)} copy(f32[2,4,40,4,40,32]{2,1,5,4,3,0:T(4,128)} %bitcast.134) | data formatting | bytes 13107200 | tf_op jit(solution)/shard_map/all_to_all | solution.py:64
  2167.2 57.2 %reduce.2 = f32[8,204800]{1,0:T(8,128)} reduce(f32[8,1,204800]{2,1,0:T(1,128)} %all-to-all-done.8, f32[]{:T(128)} %broadcast.227), dimensions={1}, to_apply=%all_to_all.170.reduce_sub_computation | reduce | bytes 13107204 | tf_op jit(solution)/shard_map/all_to_all | solution.py:60
  2290.7 57.2 %reduce.8 = f32[8,204800]{1,0:T(8,128)} reduce(f32[8,1,204800]{2,1,0:T(1,128)} %all-to-all-done.2, f32[]{:T(128)} %broadcast.227), dimensions={1}, to_apply=%all_to_all.147.reduce_sub_computation | reduce | bytes 13107204 | tf_op jit(solution)/shard_map/all_to_all | solution.py:59
  2458.9 57.0 %reduce.4 = f32[8,204800]{1,0:T(8,128)} reduce(f32[8,1,204800]{2,1,0:T(1,128)} %all-to-all-done.10, f32[]{:T(128)} %broadcast.227), dimensions={1}, to_apply=%all_to_all.177.reduce_sub_computation | reduce | bytes 13107204 | tf_op jit(solution)/shard_map/all_to_all | solution.py:77
  2515.9 27.0 reshape.229
  2566.5 57.0 %reduce.7 = f32[8,204800]{1,0:T(8,128)} reduce(f32[8,1,204800]{2,1,0:T(1,128)} %all-to-all-done.7, f32[]{:T(128)} %broadcast.227), dimensions={1}, to_apply=%all_to_all.166.reduce_sub_computation | reduce | bytes 13107204 | tf_op jit(solution)/shard_map/all_to_all | solution.py:70
  2673.7 57.2 %reduce.10 = f32[8,204800]{1,0:T(8,128)} reduce(f32[8,1,204800]{2,1,0:T(1,128)} %all-to-all-done.4, f32[]{:T(128)} %broadcast.227), dimensions={1}, to_apply=%all_to_all.154.reduce_sub_computation | reduce | bytes 13107204 | tf_op jit(solution)/shard_map/all_to_all | solution.py:63
  2781.2 65.5 %fusion.9 = (f32[1,40,32,20,32]{2,1,3,4,0:T(8,128)}, f32[1,40,32,20,32]{2,1,3,4,0:T(8,128)}) fusion(f32[2,40,32,20,32]{2,1,3,4,0:T(8,128)} %slice_bitcast_fusion, f32[1,40,32,20,32]{2,1,3,4,0:T(8,128)} %copy.164, f32[2,40,32,20,32]{2,1,3,4,0:T(8,128)} %bitcast.114, f32[2,40,32,20,32]{2,1,3,4,0:T(8,128)} %bitcast.115, ...), kind=kLoop, calls=%fused_computation.23 | loop fusion | flops 18841600 | bytes 52443392 | tf_op jit(solution)/shard_map/sub | solution.py:96
  (115 shorter events, 987.0 us)
Async XLA Ops:
  205.9 159.0 %copy-start = (f32[25600]{0:T(1024)}, f32[25600]{0:T(1024)S(1)}, u32[]{:S(2)}) copy-start(f32[25600]{0:T(1024)S(1)} %gather_fusion.1) | copy-start | bytes 307204
  206.7 158.2 %copy-start.8 = (f32[20,160]{1,0:T(8,128)S(1)}, f32[20,160]{1,0:T(8,128)}, u32[]{:S(2)}) copy-start(f32[20,160]{1,0:T(8,128)} %param.3) | copy-start | bytes 38404
  364.8 75.4 %copy-start.2 = (f32[25600]{0:T(1024)}, f32[25600]{0:T(1024)S(1)}, u32[]{:S(2)}) copy-start(f32[25600]{0:T(1024)S(1)} %gather_fusion) | copy-start | bytes 307204
  530.5 151.2 %all-to-all-start = ((f32[8,1,204800]{2,1,0:T(1,128)}), f32[8,1,204800]{2,1,0:T(1,128)}, u32[]{:S(2)}, u32[]{:S(2)}) async-start(f32[8,1,204800]{2,1,0:T(1,128)} %reshape.236), calls=%async_computation | async-start | bytes 13107200 | tf_op jit(solution)/shard_map/all_to_all | solution.py:53
  681.7 147.7 %all-to-all-start.1 = ((f32[8,1,204800]{2,1,0:T(1,128)}), f32[8,1,204800]{2,1,0:T(1,128)}, u32[]{:S(2)}, u32[]{:S(2)}) async-start(f32[8,1,204800]{2,1,0:T(1,128)} %reshape.222), calls=%async_computation.1 | async-start | bytes 13107200 | tf_op jit(solution)/shard_map/all_to_all | solution.py:52
  733.6 100.6 %copy-start.1 = (f32[25600]{0:T(1024)S(1)}, f32[25600]{0:T(1024)}, u32[]{:S(2)}) copy-start(f32[25600]{0:T(1024)} %copy-done) | copy-start | bytes 307204
  733.6 100.7 %copy-start.3 = (f32[25600]{0:T(1024)S(1)}, f32[25600]{0:T(1024)}, u32[]{:S(2)}) copy-start(f32[25600]{0:T(1024)} %copy-done.2) | copy-start | bytes 307204
  829.4 332.5 %all-to-all-start.5 = ((f32[8,1,204800]{2,1,0:T(1,128)}), f32[8,1,204800]{2,1,0:T(1,128)}, u32[]{:S(2)}, u32[]{:S(2)}) async-start(f32[8,1,204800]{2,1,0:T(1,128)} %reshape.230), calls=%async_computation.5 | async-start | bytes 13107200 | tf_op jit(solution)/shard_map/all_to_all | solution.py:54
  1039.3 53.7 %slice-start = ((s8[10485760]{0:T(1024)(128)(4,1)}), s8[4194304]{0:T(1024)(128)(4,1)S(1)}, s32[]{:S(2)}) async-start(s8[10485760]{0:T(1024)(128)(4,1)} %bitcast.146), calls=%async_computation.11 | async-start | bytes 8388608
  1039.3 53.7 %slice-start.1 = ((s8[10485760]{0:T(1024)(128)(4,1)}), s8[4194304]{0:T(1024)(128)(4,1)S(1)}, s32[]{:S(2)}) async-start(s8[10485760]{0:T(1024)(128)(4,1)} %bitcast.146), calls=%async_computation.12 | async-start | bytes 8388608
  1049.4 43.6 %slice-start.2 = ((s8[10485760]{0:T(1024)(128)(4,1)}), s8[2097152]{0:T(1024)(128)(4,1)S(1)}, s32[]{:S(2)}) async-start(s8[10485760]{0:T(1024)(128)(4,1)} %bitcast.146), calls=%async_computation.13 | async-start | bytes 4194304
  1161.8 139.8 %all-to-all-start.9 = ((f32[4,1,409600]{2,1,0:T(1,128)}), f32[4,1,409600]{2,1,0:T(1,128)}, u32[]{:S(2)}, u32[]{:S(2)}) async-start(f32[4,1,409600]{2,1,0:T(1,128)} %reshape.226), calls=%async_computation.9 | async-start | bytes 13107200 | tf_op jit(solution)/shard_map/all_to_all | solution.py:78
  1301.6 79.0 %all-to-all-start.6 = ((f32[4,1,409600]{2,1,0:T(1,128)}), f32[4,1,409600]{2,1,0:T(1,128)}, u32[]{:S(2)}, u32[]{:S(2)}) async-start(f32[4,1,409600]{2,1,0:T(1,128)} %reshape.232), calls=%async_computation.6 | async-start | bytes 13107200 | tf_op jit(solution)/shard_map/all_to_all | solution.py:71
  1380.6 78.8 %all-to-all-start.3 = ((f32[4,1,409600]{2,1,0:T(1,128)}), f32[4,1,409600]{2,1,0:T(1,128)}, u32[]{:S(2)}, u32[]{:S(2)}) async-start(f32[4,1,409600]{2,1,0:T(1,128)} %reshape.240), calls=%async_computation.3 | async-start | bytes 13107200 | tf_op jit(solution)/shard_map/all_to_all | solution.py:64
  1459.4 149.5 %all-to-all-start.8 = ((f32[8,1,204800]{2,1,0:T(1,128)}), f32[8,1,204800]{2,1,0:T(1,128)}, u32[]{:S(2)}, u32[]{:S(2)}) async-start(f32[8,1,204800]{2,1,0:T(1,128)} %reshape.224), calls=%async_computation.8 | async-start | bytes 13107200 | tf_op jit(solution)/shard_map/all_to_all | solution.py:60
  1609.0 182.7 %all-to-all-start.2 = ((f32[8,1,204800]{2,1,0:T(1,128)}), f32[8,1,204800]{2,1,0:T(1,128)}, u32[]{:S(2)}, u32[]{:S(2)}) async-start(f32[8,1,204800]{2,1,0:T(1,128)} %reshape.238), calls=%async_computation.2 | async-start | bytes 13107200 | tf_op jit(solution)/shard_map/all_to_all | solution.py:59
  1791.6 183.7 %all-to-all-start.10 = ((f32[8,1,204800]{2,1,0:T(1,128)}), f32[8,1,204800]{2,1,0:T(1,128)}, u32[]{:S(2)}, u32[]{:S(2)}) async-start(f32[8,1,204800]{2,1,0:T(1,128)} %reshape.228), calls=%async_computation.10 | async-start | bytes 13107200 | tf_op jit(solution)/shard_map/all_to_all | solution.py:77
  1975.4 183.9 %all-to-all-start.7 = ((f32[8,1,204800]{2,1,0:T(1,128)}), f32[8,1,204800]{2,1,0:T(1,128)}, u32[]{:S(2)}, u32[]{:S(2)}) async-start(f32[8,1,204800]{2,1,0:T(1,128)} %reshape.234), calls=%async_computation.7 | async-start | bytes 13107200 | tf_op jit(solution)/shard_map/all_to_all | solution.py:70
  2159.3 514.5 %all-to-all-start.4 = ((f32[8,1,204800]{2,1,0:T(1,128)}), f32[8,1,204800]{2,1,0:T(1,128)}, u32[]{:S(2)}, u32[]{:S(2)}) async-start(f32[8,1,204800]{2,1,0:T(1,128)} %reshape.242), calls=%async_computation.4 | async-start | bytes 13107200 | tf_op jit(solution)/shard_map/all_to_all | solution.py:63
  2757.6 23.6 copy-start.4
  2757.6 23.6 copy-start.5
  2757.6 23.6 copy-start.6
  2757.6 23.6 copy-start.7
where the time goes:
time: 2910 us; the launch traced here: 2900 us
  local copies, waits for them, and re-layouts  1540 us (53%)
  other arithmetic  810 us (28%)
  waiting for transfers between devices  368 us (13%)
  matrix products  119 us (4%)
  starting transfers between devices  62.1 us (2%)
    unnamed x47, local copies, waits for them, and re-layouts  627 us
    gather x6, local copies, waits for them, and re-layouts, operators(): return (kinetic_row[distance], slope_row[distance])  317 us
    all_to_all x1, waiting for transfers between devices, on_device(): lax.all_to_all(grad_two, 'row', split_axis=3, concat_axis=2, tiled=True)  121 us
    all_to_all x1, waiting for transfers between devices, on_device(): lax.all_to_all(window_part, 'row', split_axis=2, concat_axis=3, tiled=True)  95.8 us
    all_to_all x1, waiting for transfers between devices, on_device(): lax.all_to_all(applied, 'row', split_axis=2, concat_axis=3, tiled=True)  79.3 us
    dot_general x1, matrix products, on_device(): jnp.einsum('cpqbx,xe->cpebq', density, matrices, precision=highest)  75.3 us
    all_to_all x1, other arithmetic, on_device(): lax.all_to_all(full_applied, 'col', split_axis=3, concat_axis=1, tiled=True)  71.8 us
    all_to_all x1, other arithmetic, on_device(): lax.all_to_all(grad_mid, 'col', split_axis=3, concat_axis=1, tiled=True)  71.7 us
  transfers between devices with their start and end apart: 11, of which 5 were waited for; matrix products, arithmetic and copies ran while one was open for 59% of the time, Pallas kernels for 0%

commit v1 on v0

--- a/solution.py
+++ b/solution.py
@@ -6,6 +6,28 @@
 friction = 0.005
 diffusion = 0.0001
 highest = lax.Precision.HIGHEST
+
+
+def in_blocks(x, dim, size):
+    before, after = (x.shape[:dim], x.shape[dim + 1 :])
+    return jnp.moveaxis(x.reshape(*before, size, -1, *after), dim, 0)
+
+
+def joined_along(tiles, dim):
+    dims = list(tiles.shape[1:])
+    dims[dim] *= tiles.shape[0]
+    return jnp.moveaxis(tiles, 0, dim).reshape(dims)
+
+
+def swapped_with_each(x, axis, split_dim, concat_dim):
+    peers, place = (lax.axis_size(axis), lax.axis_index(axis))
+    blocks = in_blocks(x, split_dim, peers)
+    gathered = [blocks[place]]
+    for step in range(1, peers):
+        sent = blocks[place ^ step]
+        gathered.append(lax.ppermute(sent, axis, [(i, i ^ step) for i in range(peers)]))
+    blocks = jnp.stack(gathered)[place ^ jnp.arange(peers)]
+    return joined_along(blocks, concat_dim)
 
 
 def operators(grid_width):
@@ -50,7 +72,7 @@
     offset_two = rows_global - cols_global
     squared = offset_one**2 + offset_two**2
     source = lax.all_to_all(window_part, "row", split_axis=2, concat_axis=3, tiled=True)
-    applied_mid = lax.all_to_all(applied, "row", split_axis=2, concat_axis=3, tiled=True)
+    applied_mid = swapped_with_each(applied, "row", 2, 3)
     grad_mid = lax.all_to_all(grad_one, "row", split_axis=2, concat_axis=3, tiled=True)
     paired = jnp.einsum("capbq,eb->capeq", source, stacked, precision=highest)
     full_applied = applied_mid + paired[:, :, :, :grid_width]

time: 2910 us -> 3210 us (1.10)
  waiting for transfers between devices: 368 us -> 577 us
  starting transfers between devices: 62.1 us -> 189 us
  other arithmetic: 810 us -> 754 us
    ppermute x0 -> x7, waiting for transfers between devices: none -> 384 us  [swapped_with_each(): lax.ppermute(sent, axis, [(i, i ^ step) for i in range(peers)])]
    all_to_all x1, starting transfers between devices: 5.9 us -> 108 us  [on_device(): lax.all_to_all(grad_two, 'row', split_axis=3, concat_axis=2, tiled=True)]
    all_to_all x1, waiting for transfers between devices: 95.8 us -> 0.01 us  [on_device(): lax.all_to_all(window_part, 'row', split_axis=2, concat_axis=3, tiled=True)]
    all_to_all x1 -> x0, waiting for transfers between devices: 79.3 us -> none  [on_device(): lax.all_to_all(applied, 'row', split_axis=2, concat_axis=3, tiled=True)]
    all_to_all x1 -> x0, other arithmetic: 57 us -> none  [on_device(): lax.all_to_all(applied, 'row', split_axis=2, concat_axis=3, tiled=True)]
    all_to_all x3 -> x0, local copies, waits for them, and re-layouts: 36.9 us -> none  [on_device(): lax.all_to_all(applied, 'row', split_axis=2, concat_axis=3, tiled=True)]
    unnamed x47 -> x48, local copies, waits for them, and re-layouts: 627 us -> 599 us
  transfers between devices with their start and end apart: 11 -> 17, of which waited for: 5 -> 7; matrix products, arithmetic and copies ran while one was open for 59% -> 66% of each run, Pallas kernels for 0% -> 0%
where the time goes in v1:
time: 3210 us; the launch traced here: 3200 us
  local copies, waits for them, and re-layouts  1560 us (49%)
  other arithmetic  754 us (23%)
  waiting for transfers between devices  577 us (18%)
  starting transfers between devices  189 us (6%)
  matrix products  118 us (4%)
    unnamed x48, local copies, waits for them, and re-layouts  599 us
    ppermute x7, waiting for transfers between devices, swapped_with_each(): lax.ppermute(sent, axis, [(i, i ^ step) for i in range(peers)])  384 us
    gather x6, local copies, waits for them, and re-layouts, operators(): return (kinetic_row[distance], slope_row[distance])  317 us
    all_to_all x1, waiting for transfers between devices, on_device(): lax.all_to_all(grad_two, 'row', split_axis=3, concat_axis=2, tiled=True)  121 us
    all_to_all x1, starting transfers between devices, on_device(): lax.all_to_all(grad_two, 'row', split_axis=3, concat_axis=2, tiled=True)  108 us
    dot_general x1, matrix products, on_device(): jnp.einsum('cpqbx,xe->cpebq', density, matrices, precision=highest)  74.8 us
    all_to_all x1, other arithmetic, on_device(): lax.all_to_all(full_applied, 'col', split_axis=3, concat_axis=1, tiled=True)  71.6 us
    all_to_all x1, other arithmetic, on_device(): lax.all_to_all(grad_mid, 'col', split_axis=3, concat_axis=1, tiled=True)  71.6 us
  transfers between devices with their start and end apart: 17, of which 7 were waited for; matrix products, arithmetic and copies ran while one was open for 66% of the time, Pallas kernels for 0%

profile of v1, /device:TPU:0, one launch (start us, length us, event | category | flops | bytes accessed | tf_op | source)
XLA Modules:
  0.0 3195.2 jit_solution(15052647901109874781)
XLA Ops:
  0.0 46.7 %copy.148 = f32[2,40,32,20,160]{4,1,3,2,0:T(8,128)} copy(f32[2,40,32,20,160]{4,2,3,1,0:T(8,128)} %param.2) | data formatting | bytes 65536000 | tf_op args[0]
  120.3 158.1 %gather_fusion.1 = f32[25600]{0:T(1024)S(1)} fusion(f32[160]{0:T(256)S(1)} %negate_multiply_fusion, s32[25600]{0:T(1024)S(1)} %broadcast_clamp_fusion), kind=kCustom, calls=%fused_computation.1 | custom fusion | bytes 307200 | tf_op jit(solution)/shard_map/gather | solution.py:43
  279.2 158.1 %gather_fusion = f32[25600]{0:T(1024)S(1)} fusion(f32[160]{0:T(256)S(1)} %broadcast_multiply_fusion, s32[25600]{0:T(1024)S(1)} %broadcast_clamp_fusion), kind=kCustom, calls=%fused_computation | custom fusion | bytes 307200 | tf_op jit(solution)/shard_map/gather | solution.py:43
  437.5 74.8 %convolution_bitcast_fusion = f32[2,40,64,20,32]{2,1,3,4,0:T(8,128)} fusion(f32[160,32]{0,1:T(8,128)S(1)} %bitcast.186, f32[160,32]{0,1:T(8,128)S(1)} %bitcast.187, f32[2,40,32,20,160]{4,2,3,1,0:T(8,128)} %param.2), kind=kOutput, calls=%fused_computation.11 | convolution fusion | flops 6291466240 | bytes 45916160 | tf_op jit(solution)/shard_map/cpqbx,xe->cpebq/dot_general | solution.py:53
  512.3 43.2 %slice_add_fusion = (f32[2,40,32,20,32]{2,1,3,4,0:T(8,128)}, f32[2,40,32,20,32]{2,1,3,4,0:T(8,128)}) fusion(f32[2,40,64,20,32]{2,1,3,4,0:T(8,128)} %convolution_bitcast_fusion, f32[32,20]{0,1:T(8,128)S(1)} %slice_bitcast_fusion.1, f32[2,40,32,20,160]{4,1,3,2,0:T(8,128)} %copy.148), kind=kLoop, calls=%fused_computation.4 | loop fusion | flops 3276800 | bytes 32770560 | tf_op jit(solution)/shard_map/add | solution.py:58
  672.7 66.9 %collective-permute-done = f32[2,40,4,20,32]{1,4,2,3,0:T(8,128)} collective-permute-done((f32[2,40,4,20,32]{1,4,2,3,0:T(8,128)}, f32[2,40,4,20,32]{1,4,2,3,0:T(8,128)}, u32[]{:S(2)}, u32[]{:S(2)}) %collective-permute-start) | collective-permute-done | bytes 819232 | tf_op jit(solution)/shard_map/ppermute | solution.py:28
  760.5 91.9 %collective-permute-done.1 = f32[2,40,4,20,32]{1,4,2,3,0:T(8,128)} collective-permute-done((f32[2,40,4,20,32]{1,4,2,3,0:T(8,128)}, f32[2,40,4,20,32]{1,4,2,3,0:T(8,128)}, u32[]{:S(2)}, u32[]{:S(2)}) %collective-permute-start.1) | collective-permute-done | bytes 819232 | tf_op jit(solution)/shard_map/ppermute | solution.py:28
  858.7 48.7 %collective-permute-done.2 = f32[2,40,4,20,32]{1,4,2,3,0:T(8,128)} collective-permute-done((f32[2,40,4,20,32]{1,4,2,3,0:T(8,128)}, f32[2,40,4,20,32]{1,4,2,3,0:T(8,128)}, u32[]{:S(2)}, u32[]{:S(2)}) %collective-permute-start.2) | collective-permute-done | bytes 819232 | tf_op jit(solution)/shard_map/ppermute | solution.py:28
  914.8 176.2 %collective-permute-done.4 = f32[2,40,4,20,32]{1,4,2,3,0:T(8,128)} collective-permute-done((f32[2,40,4,20,32]{1,4,2,3,0:T(8,128)}, f32[2,40,4,20,32]{1,4,2,3,0:T(8,128)}, u32[]{:S(2)}, u32[]{:S(2)}) %collective-permute-start.4) | collective-permute-done | bytes 819232 | tf_op jit(solution)/shard_map/ppermute | solution.py:28
  1151.3 57.3 %reduce = f32[8,204800]{1,0:T(8,128)} reduce(f32[8,1,204800]{2,1,0:T(1,128)} %all-to-all-done, f32[]{:T(128)} %broadcast.262), dimensions={1}, to_apply=%all_to_all.126.reduce_sub_computation | reduce | bytes 13107204 | tf_op jit(solution)/shard_map/all_to_all | solution.py:74
  1245.3 43.6 %fusion.15 = f32[2,40,4,320,32]{3,1,4,2,0:T(8,128)} fusion(f32[2,40,4,160,32]{1,4,3,2,0:T(8,128)S(1)} %bitcast.149, f32[160,160]{0,1:T(8,128)S(1)} %copy.161, f32[160,160]{0,1:T(8,128)S(1)} %copy.160), kind=kOutput, calls=%fused_computation.35 | convolution fusion | flops 6291507200 | bytes 19865600 | tf_op jit(solution)/shard_map/capbq,eb->capeq/dot_general | solution.py:77
  1324.2 33.7 %reshape.273 = f32[4,1,409600]{2,1,0:T(1,128)} reshape(f32[160,2,4,32,40]{4,3,2,1,0:T(8,128)} %bitcast.145) | data formatting | bytes 13107200
  1363.3 57.0 %reduce.4 = f32[8,204800]{1,0:T(8,128)} reduce(f32[8,1,204800]{2,1,0:T(1,128)} %all-to-all-done.4, f32[]{:T(128)} %broadcast.262), dimensions={1}, to_apply=%all_to_all.141.reduce_sub_computation | reduce | bytes 13107204 | tf_op jit(solution)/shard_map/all_to_all | solution.py:76
  1464.2 33.4 %reshape.279 = f32[4,1,409600]{2,1,0:T(1,128)} reshape(f32[160,2,4,32,40]{4,3,2,1,0:T(8,128)} %bitcast.162) | data formatting | bytes 13107200
  1522.0 33.4 %reshape.285 = f32[4,1,409600]{2,1,0:T(1,128)} reshape(f32[160,2,4,32,40]{4,3,2,1,0:T(8,128)} %bitcast.147) | data formatting | bytes 13107200
  1605.1 50.6 %all-to-all-done.2 = f32[4,1,409600]{2,1,0:T(1,128)} async-done(((f32[4,1,409600]{2,1,0:T(1,128)}), f32[4,1,409600]{2,1,0:T(1,128)}, u32[]{:S(2)}, u32[]{:S(2)}) %all-to-all-start.2) | async-done | bytes 6553632 | tf_op jit(solution)/shard_map/all_to_all | solution.py:86
  1655.7 108.5 %all-to-all-start.7 = ((f32[8,1,204800]{2,1,0:T(1,128)}), f32[8,1,204800]{2,1,0:T(1,128)}, u32[]{:S(2)}, u32[]{:S(2)}) async-start(f32[8,1,204800]{2,1,0:T(1,128)} %reshape.271), calls=%async_computation.7 | async-start | bytes 13107200 | tf_op jit(solution)/shard_map/all_to_all | solution.py:82
  1787.1 121.3 %all-to-all-done.7 = f32[8,1,204800]{2,1,0:T(1,128)} async-done(((f32[8,1,204800]{2,1,0:T(1,128)}), f32[8,1,204800]{2,1,0:T(1,128)}, u32[]{:S(2)}, u32[]{:S(2)}) %all-to-all-start.7) | async-done | bytes 6553632 | tf_op jit(solution)/shard_map/all_to_all | solution.py:82
  1913.3 71.5 %reduce.2 = f32[4,409600]{1,0:T(4,128)} reduce(f32[4,1,409600]{2,1,0:T(1,128)} %all-to-all-done.8, f32[]{:T(128)} %broadcast.262), dimensions={1}, to_apply=%all_to_all.156.reduce_sub_computation | reduce | bytes 13107204 | tf_op jit(solution)/shard_map/all_to_all | solution.py:100
  1984.8 27.5 reshape.274
  2037.9 30.3 copy.206
  2097.1 71.6 %reduce.5 = f32[4,409600]{1,0:T(4,128)} reduce(f32[4,1,409600]{2,1,0:T(1,128)} %all-to-all-done.5, f32[]{:T(128)} %broadcast.262), dimensions={1}, to_apply=%all_to_all.145.reduce_sub_computation | reduce | bytes 13107204 | tf_op jit(solution)/shard_map/all_to_all | solution.py:93
  2221.8 30.2 copy.204
  2280.9 71.6 %reduce.8 = f32[4,409600]{1,0:T(4,128)} reduce(f32[4,1,409600]{2,1,0:T(1,128)} %all-to-all-done.2, f32[]{:T(128)} %broadcast.262), dimensions={1}, to_apply=%all_to_all.133.reduce_sub_computation | reduce | bytes 13107204 | tf_op jit(solution)/shard_map/all_to_all | solution.py:86
  2352.6 27.5 reshape.286
  2405.7 30.3 copy.201
  2466.8 57.0 %reduce.1 = f32[8,204800]{1,0:T(8,128)} reduce(f32[8,1,204800]{2,1,0:T(1,128)} %all-to-all-done.7, f32[]{:T(128)} %broadcast.262), dimensions={1}, to_apply=%all_to_all.153.reduce_sub_computation | reduce | bytes 13107204 | tf_op jit(solution)/shard_map/all_to_all | solution.py:82
  2590.1 57.3 %reduce.7 = f32[8,204800]{1,0:T(8,128)} reduce(f32[8,1,204800]{2,1,0:T(1,128)} %all-to-all-done.1, f32[]{:T(128)} %broadcast.262), dimensions={1}, to_apply=%all_to_all.130.reduce_sub_computation | reduce | bytes 13107204 | tf_op jit(solution)/shard_map/all_to_all | solution.py:81
  2758.5 57.1 %reduce.3 = f32[8,204800]{1,0:T(8,128)} reduce(f32[8,1,204800]{2,1,0:T(1,128)} %all-to-all-done.9, f32[]{:T(128)} %broadcast.262), dimensions={1}, to_apply=%all_to_all.160.reduce_sub_computation | reduce | bytes 13107204 | tf_op jit(solution)/shard_map/all_to_all | solution.py:99
  2866.2 57.0 %reduce.6 = f32[8,204800]{1,0:T(8,128)} reduce(f32[8,1,204800]{2,1,0:T(1,128)} %all-to-all-done.6, f32[]{:T(128)} %broadcast.262), dimensions={1}, to_apply=%all_to_all.149.reduce_sub_computation | reduce | bytes 13107204 | tf_op jit(solution)/shard_map/all_to_all | solution.py:92
  2973.5 57.3 %reduce.9 = f32[8,204800]{1,0:T(8,128)} reduce(f32[8,1,204800]{2,1,0:T(1,128)} %all-to-all-done.3, f32[]{:T(128)} %broadcast.262), dimensions={1}, to_apply=%all_to_all.137.reduce_sub_computation | reduce | bytes 13107204 | tf_op jit(solution)/shard_map/all_to_all | solution.py:85
  3081.1 65.5 %fusion.9 = (f32[1,40,32,20,32]{2,1,3,4,0:T(8,128)}, f32[1,40,32,20,32]{2,1,3,4,0:T(8,128)}) fusion(f32[2,40,32,20,32]{2,1,3,4,0:T(8,128)} %slice_bitcast_fusion, f32[1,40,32,20,32]{2,1,3,4,0:T(8,128)} %copy.192, f32[2,40,32,20,32]{2,1,3,4,0:T(8,128)} %bitcast.151, f32[2,40,32,20,32]{2,1,3,4,0:T(8,128)} %bitcast.152, ...), kind=kLoop, calls=%fused_computation.24 | loop fusion | flops 18841600 | bytes 52443392 | tf_op jit(solution)/shard_map/sub | solution.py:118
  (139 shorter events, 1079.5 us)
Async XLA Ops:
  111.4 491.2 %all-to-all-start = ((f32[8,1,204800]{2,1,0:T(1,128)}), f32[8,1,204800]{2,1,0:T(1,128)}, u32[]{:S(2)}, u32[]{:S(2)}) async-start(f32[8,1,204800]{2,1,0:T(1,128)} %reshape.269), calls=%async_computation | async-start | bytes 13107200 | tf_op jit(solution)/shard_map/all_to_all | solution.py:74
  278.4 159.0 %copy-start = (f32[25600]{0:T(1024)}, f32[25600]{0:T(1024)S(1)}, u32[]{:S(2)}) copy-start(f32[25600]{0:T(1024)S(1)} %gather_fusion.1) | copy-start | bytes 307204
  279.2 158.2 %copy-start.6 = (f32[20,160]{1,0:T(8,128)S(1)}, f32[20,160]{1,0:T(8,128)}, u32[]{:S(2)}) copy-start(f32[20,160]{1,0:T(8,128)} %param.3) | copy-start | bytes 38404
  602.6 755.3 %all-to-all-start.4 = ((f32[8,1,204800]{2,1,0:T(1,128)}), f32[8,1,204800]{2,1,0:T(1,128)}, u32[]{:S(2)}, u32[]{:S(2)}) async-start(f32[8,1,204800]{2,1,0:T(1,128)} %reshape.277), calls=%async_computation.4 | async-start | bytes 13107200 | tf_op jit(solution)/shard_map/all_to_all | solution.py:76
  644.5 18.8 copy-start.1
  648.1 91.5 %collective-permute-start = (f32[2,40,4,20,32]{1,4,2,3,0:T(8,128)}, f32[2,40,4,20,32]{1,4,2,3,0:T(8,128)}, u32[]{:S(2)}, u32[]{:S(2)}) collective-permute-start(f32[2,40,4,20,32]{1,4,2,3,0:T(8,128)} %bitcast.143), channel_id=1, source_target_pairs={{0,4},{4,0},{8,12},{12,8},{16,20},{20,16},{24,28},{28,24},{1,5},{5... | collective-permute-start | bytes 2457608 | tf_op jit(solution)/shard_map/ppermute | solution.py:28
  651.9 200.5 %collective-permute-start.1 = (f32[2,40,4,20,32]{1,4,2,3,0:T(8,128)}, f32[2,40,4,20,32]{1,4,2,3,0:T(8,128)}, u32[]{:S(2)}, u32[]{:S(2)}) collective-permute-start(f32[2,40,4,20,32]{1,4,2,3,0:T(8,128)} %bitcast.142), channel_id=1, source_target_pairs={{0,8},{4,12},{8,0},{12,4},{16,24},{20,28},{24,16},{28,20},{1,9},{5... | collective-permute-start | bytes 2457608 | tf_op jit(solution)/shard_map/ppermute | solution.py:28
  655.2 252.2 %collective-permute-start.2 = (f32[2,40,4,20,32]{1,4,2,3,0:T(8,128)}, f32[2,40,4,20,32]{1,4,2,3,0:T(8,128)}, u32[]{:S(2)}, u32[]{:S(2)}) collective-permute-start(f32[2,40,4,20,32]{1,4,2,3,0:T(8,128)} %bitcast.141), channel_id=1, source_target_pairs={{0,12},{4,8},{8,4},{12,0},{16,28},{20,24},{24,20},{28,16},{1,13},{... | collective-permute-start | bytes 2457608 | tf_op jit(solution)/shard_map/ppermute | solution.py:28
  657.0 254.1 %collective-permute-start.3 = (f32[2,40,4,20,32]{1,4,2,3,0:T(8,128)}, f32[2,40,4,20,32]{1,4,2,3,0:T(8,128)}, u32[]{:S(2)}, u32[]{:S(2)}) collective-permute-start(f32[2,40,4,20,32]{1,4,2,3,0:T(8,128)} %bitcast.140), channel_id=1, source_target_pairs={{0,16},{4,20},{8,24},{12,28},{16,0},{20,4},{24,8},{28,12},{1,17},{... | collective-permute-start | bytes 2457608 | tf_op jit(solution)/shard_map/ppermute | solution.py:28
  661.8 429.2 %collective-permute-start.4 = (f32[2,40,4,20,32]{1,4,2,3,0:T(8,128)}, f32[2,40,4,20,32]{1,4,2,3,0:T(8,128)}, u32[]{:S(2)}, u32[]{:S(2)}) collective-permute-start(f32[2,40,4,20,32]{1,4,2,3,0:T(8,128)} %bitcast.139), channel_id=1, source_target_pairs={{0,20},{4,16},{8,28},{12,24},{16,4},{20,0},{24,12},{28,8},{1,21},{... | collective-permute-start | bytes 2457608 | tf_op jit(solution)/shard_map/ppermute | solution.py:28
  739.6 355.0 %collective-permute-start.5 = (f32[2,40,4,20,32]{1,4,2,3,0:T(8,128)}, f32[2,40,4,20,32]{1,4,2,3,0:T(8,128)S(1)}, u32[]{:S(2)}, u32[]{:S(2)}) collective-permute-start(f32[2,40,4,20,32]{1,4,2,3,0:T(8,128)} %bitcast.185), channel_id=1, source_target_pairs={{0,24},{4,28},{8,16},{12,20},{16,8},{20,12},{24,0},{28,4},{1,25},{... | collective-permute-start | bytes 2457608 | tf_op jit(solution)/shard_map/ppermute | solution.py:28
  852.4 243.9 %collective-permute-start.6 = (f32[2,40,4,20,32]{1,4,2,3,0:T(8,128)}, f32[2,40,4,20,32]{1,4,2,3,0:T(8,128)S(1)}, u32[]{:S(2)}, u32[]{:S(2)}) collective-permute-start(f32[2,40,4,20,32]{1,4,2,3,0:T(8,128)} %bitcast.184), channel_id=1, source_target_pairs={{0,28},{4,24},{8,20},{12,16},{16,12},{20,8},{24,4},{28,0},{1,29},{... | collective-permute-start | bytes 2457608 | tf_op jit(solution)/shard_map/ppermute | solution.py:28
  1235.3 53.7 %slice-start = ((s8[10485760]{0:T(1024)(128)(4,1)}), s8[4194304]{0:T(1024)(128)(4,1)S(1)}, s32[]{:S(2)}) async-start(s8[10485760]{0:T(1024)(128)(4,1)} %bitcast.182), calls=%async_computation.10 | async-start | bytes 8388608
  1235.3 53.7 %slice-start.1 = ((s8[10485760]{0:T(1024)(128)(4,1)}), s8[4194304]{0:T(1024)(128)(4,1)S(1)}, s32[]{:S(2)}) async-start(s8[10485760]{0:T(1024)(128)(4,1)} %bitcast.182), calls=%async_computation.11 | async-start | bytes 8388608
  1245.3 43.6 %slice-start.2 = ((s8[10485760]{0:T(1024)(128)(4,1)}), s8[2097152]{0:T(1024)(128)(4,1)S(1)}, s32[]{:S(2)}) async-start(s8[10485760]{0:T(1024)(128)(4,1)} %bitcast.182), calls=%async_computation.12 | async-start | bytes 4194304
  1357.9 139.7 %all-to-all-start.8 = ((f32[4,1,409600]{2,1,0:T(1,128)}), f32[4,1,409600]{2,1,0:T(1,128)}, u32[]{:S(2)}, u32[]{:S(2)}) async-start(f32[4,1,409600]{2,1,0:T(1,128)} %reshape.273), calls=%async_computation.8 | async-start | bytes 13107200 | tf_op jit(solution)/shard_map/all_to_all | solution.py:100
  1497.6 79.2 %all-to-all-start.5 = ((f32[4,1,409600]{2,1,0:T(1,128)}), f32[4,1,409600]{2,1,0:T(1,128)}, u32[]{:S(2)}, u32[]{:S(2)}) async-start(f32[4,1,409600]{2,1,0:T(1,128)} %reshape.279), calls=%async_computation.5 | async-start | bytes 13107200 | tf_op jit(solution)/shard_map/all_to_all | solution.py:93
  1576.8 78.8 %all-to-all-start.2 = ((f32[4,1,409600]{2,1,0:T(1,128)}), f32[4,1,409600]{2,1,0:T(1,128)}, u32[]{:S(2)}, u32[]{:S(2)}) async-start(f32[4,1,409600]{2,1,0:T(1,128)} %reshape.285), calls=%async_computation.2 | async-start | bytes 13107200 | tf_op jit(solution)/shard_map/all_to_all | solution.py:86
  1655.7 252.7 %all-to-all-start.7 = ((f32[8,1,204800]{2,1,0:T(1,128)}), f32[8,1,204800]{2,1,0:T(1,128)}, u32[]{:S(2)}, u32[]{:S(2)}) async-start(f32[8,1,204800]{2,1,0:T(1,128)} %reshape.271), calls=%async_computation.7 | async-start | bytes 13107200 | tf_op jit(solution)/shard_map/all_to_all | solution.py:82
  1908.4 182.8 %all-to-all-start.1 = ((f32[8,1,204800]{2,1,0:T(1,128)}), f32[8,1,204800]{2,1,0:T(1,128)}, u32[]{:S(2)}, u32[]{:S(2)}) async-start(f32[8,1,204800]{2,1,0:T(1,128)} %reshape.283), calls=%async_computation.1 | async-start | bytes 13107200 | tf_op jit(solution)/shard_map/all_to_all | solution.py:81
  2091.2 183.8 %all-to-all-start.9 = ((f32[8,1,204800]{2,1,0:T(1,128)}), f32[8,1,204800]{2,1,0:T(1,128)}, u32[]{:S(2)}, u32[]{:S(2)}) async-start(f32[8,1,204800]{2,1,0:T(1,128)} %reshape.275), calls=%async_computation.9 | async-start | bytes 13107200 | tf_op jit(solution)/shard_map/all_to_all | solution.py:99
  2274.9 184.0 %all-to-all-start.6 = ((f32[8,1,204800]{2,1,0:T(1,128)}), f32[8,1,204800]{2,1,0:T(1,128)}, u32[]{:S(2)}, u32[]{:S(2)}) async-start(f32[8,1,204800]{2,1,0:T(1,128)} %reshape.281), calls=%async_computation.6 | async-start | bytes 13107200 | tf_op jit(solution)/shard_map/all_to_all | solution.py:92
  2458.9 514.6 %all-to-all-start.3 = ((f32[8,1,204800]{2,1,0:T(1,128)}), f32[8,1,204800]{2,1,0:T(1,128)}, u32[]{:S(2)}, u32[]{:S(2)}) async-start(f32[8,1,204800]{2,1,0:T(1,128)} %reshape.287), calls=%async_computation.3 | async-start | bytes 13107200 | tf_op jit(solution)/shard_map/all_to_all | solution.py:85
  3057.5 23.6 copy-start.2
  3057.5 23.6 copy-start.3
  3057.5 23.6 copy-start.4
  3057.5 23.6 copy-start.5
